TPU v7x, 128 devices: a whole 4x4x4 slice. The times are simulated.
128 devices in a mesh: lo: 4 (over x), hi: 32 (over z, y, core).
Axes of the slice: x: 4, y: 4, z: 4, core: 2. Of those that a mesh axis runs over, the one named last changes fastest.
Arguments:
- children: float32 [8192, 64, 128], P(('lo', 'hi')), may hold values from -6 to 6
- parents: float32 [8192, 64, 128], P(('lo', 'hi')), may hold values from -6 to 6
- hamiltonian: float32 [64, 64], replicated
- damping: float32 [64], replicated, may hold values from 0.2 to 2
- coupling_real: float32 [64], replicated, may hold values from 0.3 to 2
- coupling_imag: float32 [64], replicated, may hold values from -1.5 to -0.2
- child_modes: int32 [8192, 4], P(('lo', 'hi')), may hold values from 0 to 63, as said below
- child_source: int32 [8192, 4], P(('lo', 'hi')), may hold values from 0 to 319, as said below
- parent_modes: int32 [8192, 3], P(('lo', 'hi')), may hold values from 0 to 63, as said below
- send_rows: int32 [128, 128, 2], P(('lo', 'hi')), may hold values from 0 to 63
- live_count: int32 [128], P(('lo', 'hi')), may hold values from 8 to 64, as said below
Outputs:
- child_rates: float32 [8192, 64, 128], P(('lo', 'hi'))
- parent_rates: float32 [8192, 64, 128], P(('lo', 'hi'))
Inputs may be any that keep to these rules, and one draw needn't show every extreme that they name: `child_modes`: the four modes of a row are distinct. `parent_modes`: the three modes of a row are distinct. `child_source`: the slots of one device name at most 4 times values q >= 64 with one and the same e = (q - 64) // 2; on every device some e is named exactly 4 times. `live_count`: some device is full and some holds 8 live matrices.
All inputs are finite; a program needn't handle non-finite values.
Results may differ from a plain program's by a relative error of at most 0.0003.
Values sent between devices are 32-bit elements; how exact they have to be, the bound alone decides.
A program may use at most 192 MiB of HBM per device.

v0:
```python
import jax
import jax.numpy as jnp
from jax import lax
from jax.experimental import pallas as pl
from jax.experimental.pallas import tpu as pltpu
from jax.sharding import PartitionSpec as P

MESH = pl.DeviceIdType.MESH
F32 = jnp.float32
BF16 = jnp.bfloat16
I32 = jnp.int32
LANES = 128
HALF = 64
ROWS = 4096
SLOTS = 256
PLACES = 4
CHUNK = 256
DEVICES = 128
BOX = DEVICES * 2 * PLACES
REQS = DEVICES * PLACES


def iota(shape, axis):
    return lax.broadcasted_iota(I32, shape, axis)


def split(x):
    high = x.astype(BF16)
    return high, (x - high.astype(F32)).astype(BF16)


def side_by_side(x):
    return jnp.concatenate(split(x), axis=1)


def dot(a, b):
    return lax.dot_general(a, b, (((1,), (0,)), ((), ())), preferred_element_type=F32)


def dot_nt(a, b):
    return lax.dot_general(a, b, (((1,), (1,)), ((), ())), preferred_element_type=F32)


def turn(x):
    return pltpu.roll(x, HALF, 1)


def rearrange(flipped):
    left = iota((HALF, LANES), 1) < HALF
    blocks = []
    for pair in range(2):
        top = flipped[:HALF, pair * LANES : (pair + 1) * LANES]
        low = flipped[HALF:, pair * LANES : (pair + 1) * LANES]
        blocks.append(jnp.where(left, top, turn(low)))
        blocks.append(jnp.where(left, turn(top), low))
    return jnp.concatenate(blocks, axis=0)


def transposed_chunk(x):
    eye = (iota((LANES, 2 * LANES), 0) == lax.rem(iota((LANES, 2 * LANES), 1), LANES)).astype(F32).astype(BF16)
    return rearrange(dot_nt(eye, side_by_side(x)))


def column(table):
    return jnp.concatenate([table[:, s : s + 1] for s in range(4)], axis=0)


def as_row(col):
    return jnp.broadcast_to(col.astype(F32), (col.shape[0], LANES)).T[0:1, :].astype(I32)


def slot_places(source):
    q_col = column(source)
    q_row = as_row(q_col)
    far_col, far_row = q_col >= HALF, q_row >= HALF
    owner_col = jnp.where(far_col, (q_col - HALF) >> 1, -1)
    owner_row = jnp.where(far_row, (q_row - HALF) >> 1, -1)
    same = (owner_col == owner_row).astype(I32)
    down, across = iota((SLOTS, SLOTS), 0), iota((SLOTS, SLOTS), 1)
    before = jnp.where(across < down, same, 0).astype(F32)
    after = jnp.where(down < across, same, 0).astype(F32)
    rank_col = jnp.sum(before, axis=1, keepdims=True).astype(I32)
    rank_row = jnp.sum(after, axis=0, keepdims=True).astype(I32)
    return owner_col, rank_col, owner_row, rank_row


def exchange_kernel(
    modes_s, source_s, live_s, modes, source, table, children, parents,
    inbox, answers, raised_row, raised_col, near_row, near_col,
    kids, kids_t, folks, folks_t, outbox, reply, targets, targets_s,
    in_sem, local_sem, send_sem, recv_sem,
):
    lo, hi = lax.axis_index("lo"), lax.axis_index("hi")
    me = lo * 32 + hi
    get_kids = pltpu.make_async_copy(children, kids, in_sem.at[0])
    get_folks = pltpu.make_async_copy(parents, folks, in_sem.at[1])
    get_kids.start()
    get_folks.start()

    barrier = pltpu.get_barrier_semaphore()

    def greet(k, carry):
        peer = lax.rem(me + k, DEVICES)
        pl.semaphore_signal(barrier, 1, device_id=(peer // 32, lax.rem(peer, 32)), device_id_type=MESH)
        return carry

    lax.fori_loop(1, DEVICES, greet, 0)

    owner_col, rank_col, owner_row, rank_row = slot_places(source[...])
    mode_col = column(modes[...])
    q_col = column(source[...])
    place_col = lax.rem(jnp.maximum(q_col - HALF, 0), 2)
    alive_col = (lax.rem(iota((SLOTS, 1), 0), HALF) < live_s[0])

    get_kids.wait()

    def turn_kids(i, carry):
        at = pl.ds(pl.multiple_of(i * CHUNK, CHUNK), CHUNK)
        kids_t[at, :] = transposed_chunk(kids[at, :])
        return carry

    lax.fori_loop(0, ROWS // CHUNK, turn_kids, 0)

    def pick_kids(a, carry):
        for s in range(4):
            line = a * HALF + modes_s[a, s]
            raised_row[pl.ds(s * HALF + a, 1), :] = kids[pl.ds(line, 1), :]
            raised_col[pl.ds(s * HALF + a, 1), :] = kids_t[pl.ds(line, 1), :]
        return carry

    lax.fori_loop(0, HALF, pick_kids, 0, unroll=4)

    lane = iota((SLOTS, LANES), 1)
    diagonal = lax.rem(lane, HALF) == mode_col
    gone = diagonal | jnp.logical_not(alive_col)
    row = jnp.where(gone, 0.0, raised_row[...])
    col = jnp.where(gone, 0.0, raised_col[...])
    raised_row[...] = row
    raised_col[...] = col
    code = (place_col * HALF + mode_col + 1).astype(F32)
    sent = jnp.where(lane == mode_col, col[:, 0:1], col)
    sent = jnp.where(lane == 0, code, sent)
    spot_row = jnp.where(owner_row >= 0, rank_row * DEVICES + owner_row, -1)
    pick = (iota((REQS, SLOTS), 0) == spot_row).astype(F32).astype(BF16)
    row_high, row_low = split(row)
    col_high, col_low = split(sent)
    packed = dot(pick, jnp.concatenate([row_high, col_high, row_low, col_low], axis=1))
    packed = packed[:, : 2 * LANES] + packed[:, 2 * LANES :]
    for j in range(PLACES):
        part = packed[j * DEVICES : (j + 1) * DEVICES]
        outbox[pl.ds(j, DEVICES, stride=8), :] = part[:, :LANES]
        outbox[pl.ds(PLACES + j, DEVICES, stride=8), :] = part[:, LANES:]

    pl.semaphore_wait(barrier, DEVICES - 1)

    def tile(ref, d):
        return ref.at[pl.ds(pl.multiple_of(d * 8, 8), 8), :]

    def send_all(src, dst, which):
        own = pltpu.make_async_copy(tile(src, me), tile(dst, me), local_sem.at[which])
        own.start()

        def send(k, carry):
            peer = lax.rem(me + k, DEVICES)
            pltpu.make_async_remote_copy(
                src_ref=tile(src, peer),
                dst_ref=tile(dst, me),
                send_sem=send_sem.at[which],
                recv_sem=recv_sem.at[which],
                device_id=(peer // 32, lax.rem(peer, 32)),
                device_id_type=MESH,
            ).start()
            return carry

        lax.fori_loop(1, DEVICES, send, 0)
        return own

    def wait_all(own, src, dst, sem):
        whole = pl.ds(0, BOX - 8)
        if own is not None:
            own.wait()
        pltpu.make_async_copy(src.at[whole, :], dst.at[whole, :], sem).wait()

    own = send_all(outbox, inbox, 0)

    get_folks.wait()

    def turn_folks(i, carry):
        at = pl.ds(pl.multiple_of(i * CHUNK, CHUNK), CHUNK)
        folks_t[at, :] = transposed_chunk(folks[at, :])
        return carry

    lax.fori_loop(0, ROWS // CHUNK, turn_folks, 0)

    def pick_near(a, carry):
        for s in range(4):
            q = source_s[a, s]
            line = jnp.minimum(q, HALF - 1) * HALF + modes_s[a, s]
            near_row[pl.ds(s * HALF + a, 1), :] = folks[pl.ds(line, 1), :]
            near_col[pl.ds(s * HALF + a, 1), :] = folks_t[pl.ds(line, 1), :]
        return carry

    lax.fori_loop(0, HALF, pick_near, 0, unroll=4)

    wait_all(own, outbox, inbox, recv_sem.at[0])

    wanted = jnp.zeros((DEVICES, LANES), F32)
    across = iota((DEVICES, LANES), 1)
    for j in range(PLACES):
        line = request_line(inbox[pl.ds(PLACES + j, DEVICES, stride=8), :], table[...])
        wanted = jnp.where(across == j, line.astype(F32), wanted)
    targets[...] = jnp.clip(wanted.T[:8, :].astype(I32), 0, ROWS - 1)
    to_scalar = pltpu.make_async_copy(targets, targets_s, in_sem.at[2])
    to_scalar.start()
    to_scalar.wait()

    def answer(d, carry):
        for j in range(PLACES):
            line = targets_s[j, d]
            reply[pl.ds(d * 8 + j, 1), :] = folks[pl.ds(line, 1), :]
            reply[pl.ds(d * 8 + PLACES + j, 1), :] = folks_t[pl.ds(line, 1), :]
        return carry

    lax.fori_loop(0, DEVICES, answer, 0, unroll=4)
    own = send_all(reply, answers, 1)
    wait_all(None, outbox, inbox, send_sem.at[0])
    wait_all(own, reply, answers, recv_sem.at[1])
    wait_all(None, reply, answers, send_sem.at[1])


def request_line(col, table):
    code = col[:, 0:1].astype(I32)
    wanted = jnp.clip(code - 1, 0, 2 * HALF - 1)
    chosen = jnp.where(wanted >= HALF, table[:, 1:2], table[:, 0:1])
    return chosen * HALF + lax.rem(wanted, HALF)


def rates_kernel(
    modes_s, parent_modes_s, live_s, damping_s,
    modes, source, table, hamiltonian, couple, inbox, answers, raised_row, raised_col, near_row, near_col,
    children, parents,
    child_out, parent_out,
    weights, left, p_rows, p_cols, p_line, c_rows, c_cols, c_line,
):
    step = pl.program_id(0)

    @pl.when(step == 0)
    def _():
        prepare(
            live_s, modes, source, table, hamiltonian, couple, inbox, answers, raised_row, raised_col, near_row,
            near_col, weights, left, p_rows, p_cols, p_line, c_rows, c_cols, c_line,
        )

    base = step * CHUNK
    for x_ref, out, rows, cols, line, modes_ref, places in (
        (children, child_out, c_rows, c_cols, c_line, modes_s, 4),
        (parents, parent_out, p_rows, p_cols, p_line, parent_modes_s, 3),
    ):
        x = x_ref[...]
        both = side_by_side(x)
        right = dot(both, weights[...])
        right = right[:, :LANES] + right[:, LANES:]
        lefts = dot(left[...], both)
        lefts = lefts[:CHUNK] + lefts[CHUNK:]
        lefts = lefts[:, :LANES] + lefts[:, LANES:]
        count = line.shape[1]
        hot = (iota((CHUNK, count), 0) + base == line[...]).astype(F32).astype(BF16)
        more = dot(hot, rows[...])
        more = more[:, :LANES] + more[:, LANES:]
        less = dot_nt(cols[...], hot)
        less = rearrange(less[:LANES] + less[LANES:])
        part = turn(lefts - right + more - less)
        part = jnp.where(iota((CHUNK, LANES), 1) < HALF, part, -part)
        for k in range(4):
            a = step * 4 + k
            rate = damping_s[modes_ref[a, 0]]
            for s in range(1, places):
                rate = rate + damping_s[modes_ref[a, s]]
            at = slice(k * HALF, (k + 1) * HALF)
            result = part[at] - rate * x[at]
            if out is child_out:
                result = jnp.where(a < live_s[0], result, 0.0)
            out[at, :] = result


def prepare(
    live_s, modes, source, table, hamiltonian, couple, inbox, answers, raised_row, raised_col, near_row, near_col,
    weights, left, p_rows, p_cols, p_line, c_rows, c_cols, c_line,
):
    h = hamiltonian[...]
    wide = jnp.concatenate([h, h], axis=1)
    tall = jnp.concatenate([wide] * 4, axis=0)
    square = jnp.where(
        lax.rem(iota((2 * LANES, LANES), 0) // HALF, 2) == iota((2 * LANES, LANES), 1) // HALF, tall, 0.0
    )
    weights[...] = side_by_side(square)
    four = jnp.concatenate([tall, tall], axis=1)
    diag = jnp.where(iota((CHUNK, CHUNK), 0) // HALF == iota((CHUNK, CHUNK), 1) // HALF, four, 0.0)
    left[...] = jnp.concatenate(split(diag), axis=0)

    wanted = jnp.zeros((DEVICES, LANES), F32)
    across = iota((DEVICES, LANES), 1)
    for j in range(PLACES):
        row = inbox[pl.ds(j, DEVICES, stride=8), :]
        col = inbox[pl.ds(PLACES + j, DEVICES, stride=8), :]
        line = request_line(col, table[...])
        wanted = jnp.where(across == j, line.astype(F32), wanted)
        mode = lax.rem(line, HALF)
        hit = across == mode
        first = jnp.sum(jnp.where(hit, col, 0.0), axis=1, keepdims=True)
        first = jnp.where(mode == 0, 0.0, first)
        col = jnp.where(across == 0, first, jnp.where(hit, 0.0, col))
        put_lines(row, col, p_rows, p_cols, j * DEVICES)
    lines = wanted.T.astype(I32)
    for j in range(PLACES):
        p_line[:, j * DEVICES : (j + 1) * DEVICES] = lines[j : j + 1, :]
    mode_col, q_col = column(modes[...]), column(source[...])
    own_line = jnp.where(q_col < HALF, q_col * HALF + mode_col, ROWS)
    p_line[:, REQS:] = as_row(own_line)
    for k in range(2):
        at = slice(k * LANES, (k + 1) * LANES)
        put_lines(raised_row[at, :], raised_col[at, :], p_rows, p_cols, REQS + k * LANES)

    owner_col, rank_col, _, _ = slot_places(source[...])
    spot = jnp.where(owner_col >= 0, owner_col * 8 + rank_col, -8)
    spots = jnp.concatenate([spot, spot + PLACES], axis=0)
    pick = (iota((2 * SLOTS, BOX), 1) == spots).astype(F32).astype(BF16)
    got = dot(pick, side_by_side(answers[...]))
    got = got[:, :LANES] + got[:, LANES:]
    near = owner_col < 0
    row = jnp.where(near, near_row[...], got[:SLOTS])
    col = jnp.where(near, near_col[...], got[SLOTS:])
    lane = iota((SLOTS, LANES), 1)
    real = jnp.sum(jnp.where(lane == mode_col, couple[0:1, :], 0.0), axis=1, keepdims=True)
    imag = jnp.sum(jnp.where(lane == mode_col, couple[1:2, :], 0.0), axis=1, keepdims=True)
    signed = jnp.where(lane < HALF, -imag, imag)
    row = real * row + signed * turn(row)
    col = real * col - signed * turn(col)
    for k in range(2):
        at = slice(k * LANES, (k + 1) * LANES)
        put_lines(row[at], col[at], c_rows, c_cols, k * LANES)
    c_line[...] = as_row(lax.rem(iota((SLOTS, 1), 0), HALF) * HALF + mode_col)


def put_lines(row, col, rows, cols, at):
    rows[at : at + LANES, :] = side_by_side(row)
    cols[:, at : at + LANES] = jnp.concatenate(split(col.T), axis=0)


VMEM = pl.BlockSpec(memory_space=pltpu.VMEM)
SMEM = pl.BlockSpec(memory_space=pltpu.SMEM)
ANY = pl.BlockSpec(memory_space=pl.ANY)


def body(
    children, parents, hamiltonian, damping, coupling_real, coupling_imag,
    child_modes, child_source, parent_modes, send_rows, live_count,
):
    kids = children.reshape(ROWS, LANES)
    folks = parents.reshape(ROWS, LANES)
    table = send_rows[0]
    lines = jax.ShapeDtypeStruct((SLOTS, LANES), F32)
    box = jax.ShapeDtypeStruct((BOX, LANES), F32)
    inbox, answers, raised_row, raised_col, near_row, near_col = pl.pallas_call(
        exchange_kernel,
        out_shape=(box, box, lines, lines, lines, lines),
        in_specs=[SMEM, SMEM, SMEM, VMEM, VMEM, VMEM, ANY, ANY],
        out_specs=(VMEM,) * 6,
        scratch_shapes=[
            pltpu.VMEM((ROWS, LANES), F32),
            pltpu.VMEM((ROWS, LANES), F32),
            pltpu.VMEM((ROWS, LANES), F32),
            pltpu.VMEM((ROWS, LANES), F32),
            pltpu.VMEM((BOX, LANES), F32),
            pltpu.VMEM((BOX, LANES), F32),
            pltpu.VMEM((8, LANES), I32),
            pltpu.SMEM((8, LANES), I32),
            pltpu.SemaphoreType.DMA((3,)),
            pltpu.SemaphoreType.DMA((2,)),
            pltpu.SemaphoreType.DMA((2,)),
            pltpu.SemaphoreType.DMA((2,)),
        ],
        compiler_params=pltpu.CompilerParams(
            collective_id=0, has_side_effects=True, vmem_limit_bytes=32 * 2**20
        ),
    )(child_modes, child_source, live_count, child_modes, child_source, table, kids, folks)
    couple = jnp.concatenate(
        [jnp.stack([coupling_real, coupling_imag]), jnp.zeros((2, LANES - HALF), F32)], axis=1
    )
    chunk = pl.BlockSpec((CHUNK, LANES), lambda i: (i, 0))
    whole = jax.ShapeDtypeStruct((ROWS, LANES), F32)
    every = REQS + SLOTS
    child_rates, parent_rates = pl.pallas_call(
        rates_kernel,
        grid=(ROWS // CHUNK,),
        out_shape=(whole, whole),
        in_specs=[SMEM] * 4 + [VMEM] * 11 + [chunk] * 2,
        out_specs=(chunk, chunk),
        scratch_shapes=[
            pltpu.VMEM((2 * LANES, 2 * LANES), BF16),
            pltpu.VMEM((2 * CHUNK, CHUNK), BF16),
            pltpu.VMEM((every, 2 * LANES), BF16),
            pltpu.VMEM((2 * LANES, every), BF16),
            pltpu.VMEM((1, every), I32),
            pltpu.VMEM((SLOTS, 2 * LANES), BF16),
            pltpu.VMEM((2 * LANES, SLOTS), BF16),
            pltpu.VMEM((1, SLOTS), I32),
        ],
        compiler_params=pltpu.CompilerParams(vmem_limit_bytes=32 * 2**20),
    )(
        child_modes, parent_modes, live_count, damping,
        child_modes, child_source, table, hamiltonian, couple,
        inbox, answers, raised_row, raised_col, near_row, near_col, kids, folks,
    )
    return child_rates.reshape(children.shape), parent_rates.reshape(parents.shape)


def solution(mesh):
    in_specs = (
        P(("lo", "hi"), None, None),
        P(("lo", "hi"), None, None),
        P(),
        P(),
        P(),
        P(),
        P(("lo", "hi"), None),
        P(("lo", "hi"), None),
        P(("lo", "hi"), None),
        P(("lo", "hi"), None, None),
        P(("lo", "hi")),
    )
    out_specs = (P(("lo", "hi"), None, None), P(("lo", "hi"), None, None))
    return jax.shard_map(body, mesh=mesh, in_specs=in_specs, out_specs=out_specs, check_vma=False)
```

profile of v0, /device:TPU:1, one launch (start us, length us, event | category | flops | bytes accessed | tf_op | source)
XLA Modules:
  0.0 64.0 jit_solution(5000600564423639279)
XLA Ops:
  1.3 0.7 %select_maximum_fusion.couple = f32[2,128]{1,0:T(2,128)S(1)} fusion(f32[1,64]{1,0:T(1,128)} %bitcast.13, f32[1,64]{1,0:T(1,128)} %bitcast.14), kind=kLoop, calls=%fused_computation | loop fusion | flops 1024 | bytes 1536 | tf_op jit(solution)/shard_map/stack | solution.py:388
  2.0 0.8 %copy.18.modes_s.modes = s32[64,4]{1,0:T(8,128)S(1)} copy(s32[64,4]{0,1:T(4,128)} %param.17) | data formatting | bytes 2048 | tf_op args[6]
  2.7 0.8 %copy.21.source_s.source = s32[64,4]{1,0:T(8,128)S(1)} copy(s32[64,4]{0,1:T(4,128)} %param.18) | data formatting | bytes 2048 | tf_op args[7]
  3.5 0.8 %copy.19.parent_modes_s = s32[64,3]{1,0:T(8,128)S(1)} copy(s32[64,3]{0,1:T(4,128)} %param.19) | data formatting | bytes 1536 | tf_op args[8]
  4.3 0.8 %copy.13 = s32[1,128,2]{2,1,0:T(8,128)S(1)} copy(s32[1,128,2]{1,2,0:T(2,128)} %param.20) | data formatting | bytes 2048 | tf_op args[9]
  5.1 0.0 copy-start
  5.1 1.6 %copy-done = f32[64,64,128]{2,1,0:T(8,128)S(1)} copy-done((f32[64,64,128]{2,1,0:T(8,128)S(1)}, f32[64,64,128]{2,1,0:T(8,128)}, u32[]{:S(2)}) %copy-start) | copy-done | bytes 2097176
  6.6 0.0 copy-start.1
  6.6 1.6 %copy-done.1 = f32[64,64,128]{2,1,0:T(8,128)S(1)} copy-done((f32[64,64,128]{2,1,0:T(8,128)S(1)}, f32[64,64,128]{2,1,0:T(8,128)}, u32[]{:S(2)}) %copy-start.1) | copy-done | bytes 2097176
  8.2 0.0 copy-start.2
  8.2 0.0 copy-start.3
  8.2 37.5 %shard_map.122 = (f32[1024,128]{1,0:T(8,128)S(1)}, f32[1024,128]{1,0:T(8,128)S(1)}, f32[256,128]{1,0:T(8,128)S(1)}, f32[256,128]{1,0:T(8,128)S(1)}, f32[256,128]{1,0:T(8,128)S(1)}, /*index=5*/f32[256,128]{1,0:T(8,128)S(1)}) custom-call(s32[64,4]{1,0:T(8,128)S(1)} %copy.18.modes_s.modes, s32[64,4]{1,0:T(8,128)S(1)} %copy.21.source_s.source, ...), custom_call_target="tpu_custom_call" | custom-call | tf_op jit(solution)/shard_map/pallas_call | solution.py:364
  45.8 0.0 copy-done.2
  45.8 0.0 copy-done.3
  45.8 18.3 %shard_map.123 = (f32[4096,128]{1,0:T(8,128)}, f32[4096,128]{1,0:T(8,128)}) custom-call(s32[64,4]{1,0:T(8,128)S(1)} %copy.18.modes_s.modes, s32[64,3]{1,0:T(8,128)S(1)} %copy.19.parent_modes_s, s32[1]{0:T(128)S(6)} %copy.22.live_s, f32[64]{0:T(128)S(1)} %copy-done.3, s32[64,4]{1,0:T(8,128)S(1)} %copy.18.modes_s.modes, s32[64,4]{1,0:T(8,128)S(1)} %copy.21.source_s.source, ...), custom_call_target="tpu_custom_call" | custom-call | tf_op jit(solution)/shard_map/pallas_call | solution.py:393
Async XLA Ops:
  5.1 1.6 %copy-start = (f32[64,64,128]{2,1,0:T(8,128)S(1)}, f32[64,64,128]{2,1,0:T(8,128)}, u32[]{:S(2)}) copy-start(f32[64,64,128]{2,1,0:T(8,128)} %param.11) | copy-start | bytes 6291460
  6.6 1.6 %copy-start.1 = (f32[64,64,128]{2,1,0:T(8,128)S(1)}, f32[64,64,128]{2,1,0:T(8,128)}, u32[]{:S(2)}) copy-start(f32[64,64,128]{2,1,0:T(8,128)} %param.12) | copy-start | bytes 6291460
  8.2 37.5 %copy-start.2 = (f32[64,64]{1,0:T(8,128)S(1)}, f32[64,64]{1,0:T(8,128)}, u32[]{:S(2)}) copy-start(f32[64,64]{1,0:T(8,128)} %hamiltonian.1) | copy-start | bytes 49156
  8.2 37.5 %copy-start.3 = (f32[64]{0:T(128)S(1)}, f32[64]{0:T(128)}, u32[]{:S(2)}) copy-start(f32[64]{0:T(128)} %damping_s.1) | copy-start | bytes 772
where the time goes:
time: 64.3 us; the launch traced here: 64 us
  Pallas kernels  55.8 us (87%)
  local copies, waits for them, and re-layouts  6.28 us (10%)
  between operations  1.31 us (2%)
  other arithmetic  0.68 us (1%)
    pallas_call x1, Pallas kernels, body(): pl.pallas_call(exchange_kernel, out_shape=(box, box, lines, lines, lines,...  37.5 us
    pallas_call x1, Pallas kernels, body(): pl.pallas_call(rates_kernel, grid=(ROWS // CHUNK,), out_shape=(whole, who...  18.3 us
    unnamed x12, local copies, waits for them, and re-layouts  6.28 us

commit v1 on v0

v1 whole, which is shorter than its diff:
```python
import jax
import jax.numpy as jnp
from jax import lax
from jax.experimental import pallas as pl
from jax.experimental.pallas import tpu as pltpu
from jax.sharding import PartitionSpec as P

MESH = pl.DeviceIdType.MESH
F32 = jnp.float32
BF16 = jnp.bfloat16
I32 = jnp.int32
LANES = 128
HALF = 64
ROWS = 4096
SLOTS = 256
PLACES = 4
CHUNK = 256
DEVICES = 128
STRIDE = 43
BOX = DEVICES * 2 * PLACES
REQS = DEVICES * PLACES


def iota(shape, axis):
    return lax.broadcasted_iota(I32, shape, axis)


def split(x):
    high = x.astype(BF16)
    return high, (x - high.astype(F32)).astype(BF16)


def side_by_side(x):
    return jnp.concatenate(split(x), axis=1)


def dot(a, b):
    return lax.dot_general(a, b, (((1,), (0,)), ((), ())), preferred_element_type=F32)


def dot_nt(a, b):
    return lax.dot_general(a, b, (((1,), (1,)), ((), ())), preferred_element_type=F32)


def turn(x):
    return pltpu.roll(x, HALF, 1)


def rearrange(flipped):
    left = iota((HALF, LANES), 1) < HALF
    blocks = []
    for pair in range(2):
        top = flipped[:HALF, pair * LANES : (pair + 1) * LANES]
        low = flipped[HALF:, pair * LANES : (pair + 1) * LANES]
        blocks.append(jnp.where(left, top, turn(low)))
        blocks.append(jnp.where(left, turn(top), low))
    return jnp.concatenate(blocks, axis=0)


def transposed_chunk(both):
    eye = (iota((LANES, 2 * LANES), 0) == lax.rem(iota((LANES, 2 * LANES), 1), LANES)).astype(F32).astype(BF16)
    return rearrange(dot_nt(eye, both))


def slots_row(table):
    twice = jnp.concatenate([table, table], axis=1)
    left = iota((1, LANES), 1) < HALF
    return jnp.concatenate([jnp.where(left, twice[s : s + 1], twice[s + 1 : s + 2]) for s in (0, 2)], axis=1)


def as_column(row):
    wide = jnp.broadcast_to(row.astype(F32), (LANES, row.shape[1]))
    parts = [wide[:, k : k + LANES].T for k in range(0, row.shape[1], LANES)]
    return jnp.concatenate(parts, axis=0)[:, 0:1].astype(I32)


def as_row(col):
    return jnp.broadcast_to(col.astype(F32), (col.shape[0], LANES)).T[0:1, :].astype(I32)


def slot_places(q_row, q_col):
    owner_col = jnp.where(q_col >= HALF, (q_col - HALF) >> 1, -1)
    owner_row = jnp.where(q_row >= HALF, (q_row - HALF) >> 1, -1)
    same = (owner_col == owner_row).astype(I32)
    down, across = iota((SLOTS, SLOTS), 0), iota((SLOTS, SLOTS), 1)
    before = jnp.where(across < down, same, 0).astype(F32)
    after = jnp.where(down < across, same, 0).astype(F32)
    rank_col = jnp.sum(before, axis=1, keepdims=True).astype(I32)
    rank_row = jnp.sum(after, axis=0, keepdims=True).astype(I32)
    return owner_col, rank_col, owner_row, rank_row


def times_minus_i(x):
    y = turn(x)
    return jnp.where(iota(x.shape, 1) < HALF, y, -y)


def prepare_hamiltonian(hamiltonian, weights, left):
    h = hamiltonian[...]
    wide = jnp.concatenate([h, h], axis=1)
    tall = jnp.concatenate([wide] * 4, axis=0)
    down, across = iota((2 * LANES, LANES), 0), iota((2 * LANES, LANES), 1)
    lower = lax.rem(down // HALF, 2) == 1
    square = jnp.where(lower == (across < HALF), jnp.where(lower, tall, -tall), 0.0)
    weights[...] = side_by_side(square)
    high, low = split(wide)
    left[...] = jnp.concatenate([high, low], axis=1)


def own_terms(x, both, first, weights, left, damping_s, modes_s, places):
    right = dot(both, weights[...])
    right = right[:, :LANES] + right[:, LANES:]
    lefts = []
    for pair in range(2):
        a, b = (both[(2 * pair + n) * HALF : (2 * pair + n + 1) * HALF] for n in range(2))
        a = jnp.concatenate([a[:, :LANES], a[:, LANES:]], axis=0)
        b = jnp.concatenate([b[:, :LANES], b[:, LANES:]], axis=0)
        ab = jnp.concatenate([a, b], axis=1)
        product = dot(left[...], jnp.concatenate([ab, ab], axis=0))
        lefts += [product[:, :LANES], product[:, LANES:]]
    part = times_minus_i(jnp.concatenate(lefts, axis=0)) - right
    results = []
    for k in range(4):
        rate = damping_s[modes_s[0, first + k]]
        for s in range(1, places):
            rate = rate + damping_s[modes_s[s, first + k]]
        at = slice(k * HALF, (k + 1) * HALF)
        results.append(part[at] - rate * x[at])
    return jnp.concatenate(results, axis=0)


def slot_sums(rows, cols, line, base):
    hot = (iota((CHUNK, line.shape[1]), 0) + base == line[...]).astype(F32).astype(BF16)
    more = dot(hot, rows[...])
    less = dot_nt(cols[...], hot)
    return more[:, :LANES] + more[:, LANES:] + rearrange(less[:LANES] + less[LANES:])


def put_lines(row, col, rows, cols, at):
    rows[at : at + LANES, :] = side_by_side(times_minus_i(row))
    cols[:, at : at + LANES] = jnp.concatenate(split(-times_minus_i(col).T), axis=0)


def exchange_kernel(
    modes_s, source_s, parent_modes_s, live_s, damping_s, modes, source, table, hamiltonian, children, parents,
    answers, near_row, near_col, kids_out, folks_out,
    kids, kids_t, folks, folks_t, kids_part, folks_done, outbox, inbox, reply, raised_row, raised_col, targets, targets_s,
    weights, left, rows, cols, lines,
    in_sem, out_sem, local_sem, send_sem, recv_sem,
):
    lo, hi = lax.axis_index("lo"), lax.axis_index("hi")
    me = lo * 32 + hi
    get_kids = pltpu.make_async_copy(children, kids, in_sem.at[0])
    get_folks = pltpu.make_async_copy(parents, folks, in_sem.at[1])
    get_kids.start()
    get_folks.start()

    barrier = pltpu.get_barrier_semaphore()

    def greet(k, carry):
        peer = lax.rem(me + k, DEVICES)
        pl.semaphore_signal(barrier, 1, device_id=(peer // 32, lax.rem(peer, 32)), device_id_type=MESH)
        return carry

    lax.fori_loop(1, DEVICES, greet, 0)

    q_row, mode_row = slots_row(source[...]), slots_row(modes[...])
    q_col, mode_col = as_column(q_row), as_column(mode_row)
    _, _, owner_row, rank_row = slot_places(q_row, q_col)
    place_col = lax.rem(jnp.maximum(q_col - HALF, 0), 2)
    alive_col = lax.rem(iota((SLOTS, 1), 0), HALF) < live_s[0]

    get_kids.wait()

    def turn_kids(i, carry):
        at = pl.ds(pl.multiple_of(i * CHUNK, CHUNK), CHUNK)
        kids_t[at, :] = transposed_chunk(side_by_side(kids[at, :]))
        return carry

    lax.fori_loop(0, ROWS // CHUNK, turn_kids, 0, unroll=2)

    def pick_kids(a, carry):
        for s in range(4):
            line = a * HALF + modes_s[s, a]
            raised_row[pl.ds(s * HALF + a, 1), :] = kids[pl.ds(line, 1), :]
            raised_col[pl.ds(s * HALF + a, 1), :] = kids_t[pl.ds(line, 1), :]
        return carry

    lax.fori_loop(0, HALF, pick_kids, 0, unroll=4)

    lane = iota((SLOTS, LANES), 1)
    diagonal = lax.rem(lane, HALF) == mode_col
    gone = diagonal | jnp.logical_not(alive_col)
    row = jnp.where(gone, 0.0, raised_row[...])
    col = jnp.where(gone, 0.0, raised_col[...])
    raised_row[...] = row
    raised_col[...] = col
    code = (place_col * HALF + mode_col + 1).astype(F32)
    sent = jnp.where(lane == mode_col, col[:, 0:1], col)
    sent = jnp.where(lane == 0, code, sent)
    spot_row = jnp.where(owner_row >= 0, rank_row * DEVICES + owner_row, -1)
    pick = (iota((REQS, SLOTS), 0) == spot_row).astype(F32).astype(BF16)
    row_high, row_low = split(row)
    col_high, col_low = split(sent)
    packed = dot(pick, jnp.concatenate([row_high, col_high, row_low, col_low], axis=1))
    packed = packed[:, : 2 * LANES] + packed[:, 2 * LANES :]
    for j in range(PLACES):
        part = packed[j * DEVICES : (j + 1) * DEVICES]
        outbox[pl.ds(j, DEVICES, stride=8), :] = part[:, :LANES]
        outbox[pl.ds(PLACES + j, DEVICES, stride=8), :] = part[:, LANES:]

    pl.semaphore_wait(barrier, DEVICES - 1)

    def tile(ref, d):
        return ref.at[pl.ds(pl.multiple_of(d * 8, 8), 8), :]

    def send(src, dst, which, peer):
        pltpu.make_async_remote_copy(
            src_ref=tile(src, peer),
            dst_ref=tile(dst, me),
            send_sem=send_sem.at[which],
            recv_sem=recv_sem.at[which],
            device_id=(peer // 32, lax.rem(peer, 32)),
            device_id_type=MESH,
        ).start()

    def keep(src, dst, which):
        return pltpu.make_async_copy(tile(src, me), tile(dst, me), local_sem.at[which])

    def wait_others(src, dst, sem):
        others = pl.ds(0, BOX - 8)
        pltpu.make_async_copy(src.at[others, :], dst.at[others, :], sem).wait()

    keep(outbox, inbox, 0).start()
    prepare_hamiltonian(hamiltonian, weights, left)
    get_folks.wait()

    def first_wait(i, carry):
        for n in range(8):
            peer = lax.rem(me + (i * 8 + n + 1) * STRIDE, DEVICES)
            if n < 7:
                send(outbox, inbox, 0, peer)
            else:
                @pl.when(i < 15)
                def _():
                    send(outbox, inbox, 0, peer)
        at = pl.ds(pl.multiple_of(i * CHUNK, CHUNK), CHUNK)
        x = folks[at, :]
        both = side_by_side(x)
        folks_t[at, :] = transposed_chunk(both)
        folks_done[at, :] = own_terms(x, both, i * 4, weights, left, damping_s, parent_modes_s, 3)
        x = kids[at, :]
        kids_part[at, :] = own_terms(x, side_by_side(x), i * 4, weights, left, damping_s, modes_s, 4)
        pltpu.make_async_copy(kids_part.at[at, :], kids_out.at[at, :], out_sem.at[0]).start()
        return carry

    lax.fori_loop(0, ROWS // CHUNK, first_wait, 0)

    def pick_near(a, carry):
        for s in range(4):
            line = jnp.minimum(source_s[s, a], HALF - 1) * HALF + modes_s[s, a]
            near_row[pl.ds(s * HALF + a, 1), :] = folks[pl.ds(line, 1), :]
            near_col[pl.ds(s * HALF + a, 1), :] = folks_t[pl.ds(line, 1), :]
        return carry

    lax.fori_loop(0, HALF, pick_near, 0, unroll=4)

    lines[:, REQS:] = jnp.where(q_row < HALF, q_row * HALF + mode_row, ROWS)
    for k in range(2):
        at = slice(k * LANES, (k + 1) * LANES)
        put_lines(raised_row[at, :], raised_col[at, :], rows, cols, REQS + k * LANES)

    keep(outbox, inbox, 0).wait()
    wait_others(outbox, inbox, recv_sem.at[0])

    codes = jnp.zeros((DEVICES, LANES), F32)
    across = iota((DEVICES, LANES), 1)
    for j in range(PLACES):
        codes = jnp.where(across == j, inbox[pl.ds(PLACES + j, DEVICES, stride=8), 0:1], codes)
    codes = jnp.clip(codes.T[:8, :].astype(I32) - 1, 0, 2 * HALF - 1)
    chosen = jnp.where(codes >= HALF, table[1:2, :], table[0:1, :])
    wanted = jnp.clip(chosen * HALF + lax.rem(codes, HALF), 0, ROWS - 1)
    targets[...] = wanted
    to_scalar = pltpu.make_async_copy(targets, targets_s, in_sem.at[2])
    to_scalar.start()

    to_scalar.wait()

    def answer(i, carry):
        for n in range(8):
            peer = lax.rem(me + (i * 8 + n + 1) * STRIDE, DEVICES)
            for j in range(PLACES):
                line = targets_s[j, peer]
                reply[pl.ds(peer * 8 + j, 1), :] = folks[pl.ds(line, 1), :]
                reply[pl.ds(peer * 8 + PLACES + j, 1), :] = folks_t[pl.ds(line, 1), :]
            if n < 7:
                send(reply, answers, 1, peer)
            else:
                @pl.when(i < 15)
                def _():
                    send(reply, answers, 1, peer)
        return carry

    lax.fori_loop(0, ROWS // CHUNK, answer, 0)
    keep(reply, answers, 1).start()

    for j in range(PLACES):
        row = inbox[pl.ds(j, DEVICES, stride=8), :]
        col = inbox[pl.ds(PLACES + j, DEVICES, stride=8), :]
        mode = lax.rem(jnp.maximum(col[:, 0:1].astype(I32) - 1, 0), HALF)
        hit = across == mode
        first = jnp.sum(jnp.where(hit, col, 0.0), axis=1, keepdims=True)
        first = jnp.where(mode == 0, 0.0, first)
        col = jnp.where(across == 0, first, jnp.where(hit, 0.0, col))
        put_lines(row, col, rows, cols, j * DEVICES)
        lines[:, j * DEVICES : (j + 1) * DEVICES] = wanted[j : j + 1, :]

    def add_raised(i, carry):
        base = pl.multiple_of(i * CHUNK, CHUNK)
        at = pl.ds(base, CHUNK)
        folks_done[at, :] = folks_done[at, :] + slot_sums(rows, cols, lines, base)
        pltpu.make_async_copy(folks_done.at[at, :], folks_out.at[at, :], out_sem.at[1]).start()
        return carry

    lax.fori_loop(0, ROWS // CHUNK, add_raised, 0, unroll=2)
    wait_others(outbox, inbox, send_sem.at[0])
    wait_others(reply, answers, send_sem.at[1])
    pltpu.make_async_copy(kids_part, kids_out, out_sem.at[0]).wait()
    pltpu.make_async_copy(folks_done, folks_out, out_sem.at[1]).wait()
    keep(reply, answers, 1).wait()
    wait_others(reply, answers, recv_sem.at[1])


def rates_kernel(
    live_s, modes, source, real, imag, answers, near_row, near_col, kids_part, folks_done,
    child_out, parent_out,
    part, done, through, rows, cols, lines, in_sem, out_sem,
):
    get_part = pltpu.make_async_copy(kids_part, part, in_sem.at[0])
    get_part.start()
    get_parents = pltpu.make_async_copy(folks_done, through, in_sem.at[1])
    get_parents.start()
    put_parents = pltpu.make_async_copy(through, parent_out, out_sem.at[0])

    q_row, mode_row = slots_row(source[...]), slots_row(modes[...])
    q_col, mode_col = as_column(q_row), as_column(mode_row)
    owner_col, rank_col, _, _ = slot_places(q_row, q_col)
    spot = jnp.where(owner_col >= 0, owner_col * 8 + rank_col, -8)
    spots = jnp.concatenate([spot, spot + PLACES], axis=0)
    pick = (iota((2 * SLOTS, BOX), 1) == spots).astype(F32).astype(BF16)
    got = dot(pick, side_by_side(answers[...]))
    got = got[:, :LANES] + got[:, LANES:]
    near = owner_col < 0
    row = jnp.where(near, near_row[...], got[:SLOTS])
    col = jnp.where(near, near_col[...], got[SLOTS:])
    lane = iota((SLOTS, LANES), 1)
    chosen = iota((SLOTS, HALF), 1) == mode_col
    factor = jnp.sum(jnp.where(chosen, real[...], 0.0), axis=1, keepdims=True)
    other = jnp.sum(jnp.where(chosen, imag[...], 0.0), axis=1, keepdims=True)
    signed = jnp.where(lane < HALF, -other, other)
    row = factor * row + signed * turn(row)
    col = factor * col - signed * turn(col)
    for k in range(2):
        at = slice(k * LANES, (k + 1) * LANES)
        put_lines(row[at], col[at], rows, cols, k * LANES)
    lines[...] = lax.rem(iota((1, SLOTS), 1), HALF) * HALF + mode_row
    limit = live_s[0] * HALF
    get_part.wait()
    get_parents.wait()
    put_parents.start()

    def add(i, carry):
        base = pl.multiple_of(i * CHUNK, CHUNK)
        at = pl.ds(base, CHUNK)
        result = part[at, :] + slot_sums(rows, cols, lines, base)
        alive = iota((CHUNK, LANES), 0) + base < limit
        done[at, :] = jnp.where(alive, result, 0.0)
        pltpu.make_async_copy(done.at[at, :], child_out.at[at, :], out_sem.at[1]).start()
        return carry

    lax.fori_loop(0, ROWS // CHUNK, add, 0, unroll=2)
    pltpu.make_async_copy(done, child_out, out_sem.at[1]).wait()
    put_parents.wait()


VMEM = pl.BlockSpec(memory_space=pltpu.VMEM)
SMEM = pl.BlockSpec(memory_space=pltpu.SMEM)
HBM = pl.BlockSpec(memory_space=pltpu.HBM)


def body(
    children, parents, hamiltonian, damping, coupling_real, coupling_imag,
    child_modes, child_source, parent_modes, send_rows, live_count,
):
    modes, source, parent_modes = child_modes.T, child_source.T, parent_modes.T
    lines = jax.ShapeDtypeStruct((SLOTS, LANES), F32)
    box = jax.ShapeDtypeStruct((BOX, LANES), F32)
    whole = jax.ShapeDtypeStruct((ROWS, LANES), F32)
    every = REQS + SLOTS
    answers, near_row, near_col, kids_part, folks_done = pl.pallas_call(
        exchange_kernel,
        out_shape=(box, lines, lines, whole, whole),
        in_specs=[SMEM] * 5 + [VMEM] * 4 + [HBM] * 2,
        out_specs=(HBM, VMEM, VMEM, HBM, HBM),
        scratch_shapes=[pltpu.VMEM((ROWS, LANES), F32)] * 6
        + [pltpu.VMEM((BOX, LANES), F32)] * 3
        + [pltpu.VMEM((SLOTS, LANES), F32)] * 2
        + [
            pltpu.VMEM((8, LANES), I32),
            pltpu.SMEM((8, LANES), I32),
            pltpu.VMEM((2 * LANES, 2 * LANES), BF16),
            pltpu.VMEM((HALF, 2 * LANES), BF16),
            pltpu.VMEM((every, 2 * LANES), BF16),
            pltpu.VMEM((2 * LANES, every), BF16),
            pltpu.VMEM((1, every), I32),
            pltpu.SemaphoreType.DMA((3,)),
            pltpu.SemaphoreType.DMA((2,)),
            pltpu.SemaphoreType.DMA((2,)),
            pltpu.SemaphoreType.DMA((2,)),
            pltpu.SemaphoreType.DMA((2,)),
        ],
        compiler_params=pltpu.CompilerParams(
            collective_id=0, has_side_effects=True, vmem_limit_bytes=60 * 2**20
        ),
    )(
        modes, source, parent_modes, live_count, damping, modes, source, send_rows[0].T, hamiltonian,
        children.reshape(ROWS, LANES), parents.reshape(ROWS, LANES),
    )
    child_rates, parent_rates = pl.pallas_call(
        rates_kernel,
        out_shape=(whole, whole),
        in_specs=[SMEM] + [VMEM] * 7 + [HBM] * 2,
        out_specs=(HBM, HBM),
        scratch_shapes=[
            pltpu.VMEM((ROWS, LANES), F32),
            pltpu.VMEM((ROWS, LANES), F32),
            pltpu.VMEM((ROWS, LANES), F32),
            pltpu.VMEM((SLOTS, 2 * LANES), BF16),
            pltpu.VMEM((2 * LANES, SLOTS), BF16),
            pltpu.VMEM((1, SLOTS), I32),
            pltpu.SemaphoreType.DMA((2,)),
            pltpu.SemaphoreType.DMA((2,)),
        ],
        compiler_params=pltpu.CompilerParams(vmem_limit_bytes=60 * 2**20),
    )(
        live_count, modes, source, coupling_real.reshape(1, HALF), coupling_imag.reshape(1, HALF),
        answers, near_row, near_col, kids_part, folks_done,
    )
    return child_rates.reshape(children.shape), parent_rates.reshape(parents.shape)


def solution(mesh):
    in_specs = (
        P(("lo", "hi"), None, None),
        P(("lo", "hi"), None, None),
        P(),
        P(),
        P(),
        P(),
        P(("lo", "hi"), None),
        P(("lo", "hi"), None),
        P(("lo", "hi"), None),
        P(("lo", "hi"), None, None),
        P(("lo", "hi")),
    )
    out_specs = (P(("lo", "hi"), None, None), P(("lo", "hi"), None, None))
    return jax.shard_map(body, mesh=mesh, in_specs=in_specs, out_specs=out_specs, check_vma=False)
```

time: 64.3 us -> 46.6 us (0.72)
  Pallas kernels: 55.8 us -> 45.1 us
  local copies, waits for them, and re-layouts: 6.28 us -> 0 us
  other arithmetic: 0.68 us -> 0 us
    pallas_call x2, Pallas kernels: 55.8 us -> 45.1 us  [the longest x1 37.8 us: body(): pl.pallas_call(exchange_kernel, out_shape=(box, lines, lines, whole, whol...]
    unnamed x12 -> x0, local copies, waits for them, and re-layouts: 6.28 us -> none
    another operation x1 -> x0, other arithmetic: 0.68 us -> none  [body(): jnp.stack([coupling_real, coupling_imag])]
where the time goes in v1:
time: 46.6 us; the launch traced here: 46.4 us
  Pallas kernels  45.1 us (97%)
  between operations  1.29 us (3%)
    pallas_call x1, Pallas kernels, body(): pl.pallas_call(exchange_kernel, out_shape=(box, lines, lines, whole, whol...  37.8 us
    pallas_call x1, Pallas kernels, body(): pl.pallas_call(rates_kernel, out_shape=(whole, whole), in_specs=[SMEM] +...  7.34 us

profile of v1, /device:TPU:1, one launch (start us, length us, event | category | flops | bytes accessed | tf_op | source)
XLA Modules:
  0.0 46.4 jit_solution(5955351458850044632)
XLA Ops:
  1.3 37.8 %shard_map.122 = (f32[1024,128]{1,0:T(8,128)}, f32[256,128]{1,0:T(8,128)}, f32[256,128]{1,0:T(8,128)}, f32[4096,128]{1,0:T(8,128)}, f32[4096,128]{1,0:T(8,128)}) custom-call(s32[4,64]{1,0:T(4,128)} %bitcast.14, s32[4,64]{1,0:T(4,128)} %bitcast.17, s32[3,64]{1,0:T(4,128)} %bitcast.20, s32[1]{0:T(128)S(6)} %copy.13.live_s, f32[64]{0:T(128)} %damping_s.1, ...), custom_call_target="tpu_custom_call" | custom-call | tf_op jit(solution)/shard_map/pallas_call | solution.py:400
  39.1 7.3 %shard_map.123 = (f32[4096,128]{1,0:T(8,128)}, f32[4096,128]{1,0:T(8,128)}) custom-call(s32[1]{0:T(128)S(6)} %copy.13.live_s, s32[4,64]{1,0:T(4,128)} %bitcast.16, s32[4,64]{1,0:T(4,128)} %bitcast.19, f32[1,64]{1,0:T(1,128)} %bitcast.22, f32[1,64]{1,0:T(1,128)} %bitcast.23, f32[1024,128]{1,0:T(8,128)} %get-tuple-element.9.answers, ...), custom_call_target="tpu_custom_call" | custom-call | tf_op jit(solution)/shard_map/pallas_call | solution.py:429

commit v2 on v1

--- a/solution.py
+++ b/solution.py
@@ -5,7 +5,7 @@
 from jax.experimental.pallas import tpu as pltpu
 from jax.sharding import PartitionSpec as P
 
-MESH = pl.DeviceIdType.MESH
+LOGICAL = pl.DeviceIdType.LOGICAL
 F32 = jnp.float32
 BF16 = jnp.bfloat16
 I32 = jnp.int32
@@ -153,13 +153,12 @@
     get_kids = pltpu.make_async_copy(children, kids, in_sem.at[0])
     get_folks = pltpu.make_async_copy(parents, folks, in_sem.at[1])
     get_kids.start()
-    get_folks.start()
 
     barrier = pltpu.get_barrier_semaphore()
 
     def greet(k, carry):
         peer = lax.rem(me + k, DEVICES)
-        pl.semaphore_signal(barrier, 1, device_id=(peer // 32, lax.rem(peer, 32)), device_id_type=MESH)
+        pl.semaphore_signal(barrier, 1, device_id=peer, device_id_type=LOGICAL)
         return carry
 
     lax.fori_loop(1, DEVICES, greet, 0)
@@ -171,13 +170,14 @@
     alive_col = lax.rem(iota((SLOTS, 1), 0), HALF) < live_s[0]
 
     get_kids.wait()
+    get_folks.start()
 
     def turn_kids(i, carry):
         at = pl.ds(pl.multiple_of(i * CHUNK, CHUNK), CHUNK)
         kids_t[at, :] = transposed_chunk(side_by_side(kids[at, :]))
         return carry
 
-    lax.fori_loop(0, ROWS // CHUNK, turn_kids, 0, unroll=2)
+    lax.fori_loop(0, ROWS // CHUNK, turn_kids, 0, unroll=4)
 
     def pick_kids(a, carry):
         for s in range(4):
@@ -220,9 +220,18 @@
             dst_ref=tile(dst, me),
             send_sem=send_sem.at[which],
             recv_sem=recv_sem.at[which],
-            device_id=(peer // 32, lax.rem(peer, 32)),
-            device_id_type=MESH,
+            device_id=peer,
+            device_id_type=LOGICAL,
         ).start()
+
+    def chunks(work):
+        def body(i, carry):
+            work(i, 8)
+            return carry
+
+        last = ROWS // CHUNK - 1
+        lax.fori_loop(0, last, body, 0, unroll=3)
+        work(last, 7)
 
     def keep(src, dst, which):
         return pltpu.make_async_copy(tile(src, me), tile(dst, me), local_sem.at[which])
@@ -235,15 +244,9 @@
     prepare_hamiltonian(hamiltonian, weights, left)
     get_folks.wait()
 
-    def first_wait(i, carry):
-        for n in range(8):
-            peer = lax.rem(me + (i * 8 + n + 1) * STRIDE, DEVICES)
-            if n < 7:
-                send(outbox, inbox, 0, peer)
-            else:
-                @pl.when(i < 15)
-                def _():
-                    send(outbox, inbox, 0, peer)
+    def first_wait(i, count):
+        for n in range(count):
+            send(outbox, inbox, 0, lax.rem(me + (i * 8 + n + 1) * STRIDE, DEVICES))
         at = pl.ds(pl.multiple_of(i * CHUNK, CHUNK), CHUNK)
         x = folks[at, :]
         both = side_by_side(x)
@@ -252,9 +255,8 @@
         x = kids[at, :]
         kids_part[at, :] = own_terms(x, side_by_side(x), i * 4, weights, left, damping_s, modes_s, 4)
         pltpu.make_async_copy(kids_part.at[at, :], kids_out.at[at, :], out_sem.at[0]).start()
-        return carry
-
-    lax.fori_loop(0, ROWS // CHUNK, first_wait, 0)
+
+    chunks(first_wait)
 
     def pick_near(a, carry):
         for s in range(4):
@@ -286,22 +288,17 @@
 
     to_scalar.wait()
 
-    def answer(i, carry):
-        for n in range(8):
-            peer = lax.rem(me + (i * 8 + n + 1) * STRIDE, DEVICES)
+    def answer(i, count):
+        peers = [lax.rem(me + (i * 8 + n + 1) * STRIDE, DEVICES) for n in range(8)]
+        for peer in peers:
             for j in range(PLACES):
                 line = targets_s[j, peer]
                 reply[pl.ds(peer * 8 + j, 1), :] = folks[pl.ds(line, 1), :]
                 reply[pl.ds(peer * 8 + PLACES + j, 1), :] = folks_t[pl.ds(line, 1), :]
-            if n < 7:
-                send(reply, answers, 1, peer)
-            else:
-                @pl.when(i < 15)
-                def _():
-                    send(reply, answers, 1, peer)
-        return carry
-
-    lax.fori_loop(0, ROWS // CHUNK, answer, 0)
+        for peer in peers[:count]:
+            send(reply, answers, 1, peer)
+
+    chunks(answer)
     keep(reply, answers, 1).start()
 
     for j in range(PLACES):
@@ -322,7 +319,7 @@
         pltpu.make_async_copy(folks_done.at[at, :], folks_out.at[at, :], out_sem.at[1]).start()
         return carry
 
-    lax.fori_loop(0, ROWS // CHUNK, add_raised, 0, unroll=2)
+    lax.fori_loop(0, ROWS // CHUNK, add_raised, 0, unroll=4)
     wait_others(outbox, inbox, send_sem.at[0])
     wait_others(reply, answers, send_sem.at[1])
     pltpu.make_async_copy(kids_part, kids_out, out_sem.at[0]).wait()
@@ -378,7 +375,7 @@
         pltpu.make_async_copy(done.at[at, :], child_out.at[at, :], out_sem.at[1]).start()
         return carry
 
-    lax.fori_loop(0, ROWS // CHUNK, add, 0, unroll=2)
+    lax.fori_loop(0, ROWS // CHUNK, add, 0, unroll=4)
     pltpu.make_async_copy(done, child_out, out_sem.at[1]).wait()
     put_parents.wait()
 

time: 46.6 us -> 45.1 us (0.968)
  Pallas kernels: 45.1 us -> 43.6 us
    pallas_call x1, Pallas kernels: 7.34 us -> 6.28 us  [body(): pl.pallas_call(rates_kernel, out_shape=(whole, whole), in_specs=[SMEM] +...]
    pallas_call x1, Pallas kernels: 37.8 us -> 37.3 us  [body(): pl.pallas_call(exchange_kernel, out_shape=(box, lines, lines, whole, whol...]
where the time goes in v2:
time: 45.1 us; the launch traced here: 44.9 us
  Pallas kernels  43.6 us (97%)
  between operations  1.29 us (3%)
    pallas_call x1, Pallas kernels, body(): pl.pallas_call(exchange_kernel, out_shape=(box, lines, lines, whole, whol...  37.3 us
    pallas_call x1, Pallas kernels, body(): pl.pallas_call(rates_kernel, out_shape=(whole, whole), in_specs=[SMEM] +...  6.28 us

profile of v2, /device:TPU:1, one launch (start us, length us, event | category | flops | bytes accessed | tf_op | source)
XLA Modules:
  0.0 44.9 jit_solution(14438050436031033837)
XLA Ops:
  1.3 37.3 %shard_map.122 = (f32[1024,128]{1,0:T(8,128)}, f32[256,128]{1,0:T(8,128)}, f32[256,128]{1,0:T(8,128)}, f32[4096,128]{1,0:T(8,128)}, f32[4096,128]{1,0:T(8,128)}) custom-call(s32[4,64]{1,0:T(4,128)} %bitcast.14, s32[4,64]{1,0:T(4,128)} %bitcast.17, s32[3,64]{1,0:T(4,128)} %bitcast.20, s32[1]{0:T(128)S(6)} %copy.13.live_s, f32[64]{0:T(128)} %damping_s.1, ...), custom_call_target="tpu_custom_call" | custom-call | tf_op jit(solution)/shard_map/pallas_call | solution.py:397
  38.6 6.3 %shard_map.123 = (f32[4096,128]{1,0:T(8,128)}, f32[4096,128]{1,0:T(8,128)}) custom-call(s32[1]{0:T(128)S(6)} %copy.13.live_s, s32[4,64]{1,0:T(4,128)} %bitcast.16, s32[4,64]{1,0:T(4,128)} %bitcast.19, f32[1,64]{1,0:T(1,128)} %bitcast.22, f32[1,64]{1,0:T(1,128)} %bitcast.23, f32[1024,128]{1,0:T(8,128)} %get-tuple-element.9.answers, ...), custom_call_target="tpu_custom_call" | custom-call | tf_op jit(solution)/shard_map/pallas_call | solution.py:426

commit v3 on v2

--- a/solution.py
+++ b/solution.py
@@ -142,17 +142,29 @@
 
 
 def exchange_kernel(
-    modes_s, source_s, parent_modes_s, live_s, damping_s, modes, source, table, hamiltonian, children, parents,
-    answers, near_row, near_col, kids_out, folks_out,
-    kids, kids_t, folks, folks_t, kids_part, folks_done, outbox, inbox, reply, raised_row, raised_col, targets, targets_s,
+    modes_s, source_s, parent_modes_s, live_s, damping_s, modes_h, source_h, table_h, hamiltonian_h, children, parents,
+    answers, near_row_out, near_col_out, kids_out, folks_out,
+    kids, kids_t, folks, folks_t, kids_part, folks_done, outbox, inbox, reply,
+    raised_row, raised_col, near_row, near_col, modes, source, table, hamiltonian, targets, targets_s,
     weights, left, rows, cols, lines,
-    in_sem, out_sem, local_sem, send_sem, recv_sem,
+    in_sem, small_sem, kids_sem, out_sem, local_sem, send_sem, recv_sem,
 ):
     lo, hi = lax.axis_index("lo"), lax.axis_index("hi")
     me = lo * 32 + hi
-    get_kids = pltpu.make_async_copy(children, kids, in_sem.at[0])
+    quarter = ROWS // 4
+    get_kids = []
+    for k in range(4):
+        at = pl.ds(k * quarter, quarter)
+        get_kids.append(pltpu.make_async_copy(children.at[at, :], kids.at[at, :], kids_sem.at[k]))
+    get_small = [
+        pltpu.make_async_copy(src, dst, small_sem.at[k])
+        for k, (src, dst) in enumerate(
+            ((modes_h, modes), (source_h, source), (table_h, table), (hamiltonian_h, hamiltonian))
+        )
+    ]
     get_folks = pltpu.make_async_copy(parents, folks, in_sem.at[1])
-    get_kids.start()
+    for copy in get_small[:2] + get_kids + get_small[2:]:
+        copy.start()
 
     barrier = pltpu.get_barrier_semaphore()
 
@@ -162,6 +174,9 @@
         return carry
 
     lax.fori_loop(1, DEVICES, greet, 0)
+    get_folks.start()
+    for copy in get_small[:2]:
+        copy.wait()
 
     q_row, mode_row = slots_row(source[...]), slots_row(modes[...])
     q_col, mode_col = as_column(q_row), as_column(mode_row)
@@ -169,15 +184,15 @@
     place_col = lax.rem(jnp.maximum(q_col - HALF, 0), 2)
     alive_col = lax.rem(iota((SLOTS, 1), 0), HALF) < live_s[0]
 
-    get_kids.wait()
-    get_folks.start()
 
     def turn_kids(i, carry):
         at = pl.ds(pl.multiple_of(i * CHUNK, CHUNK), CHUNK)
         kids_t[at, :] = transposed_chunk(side_by_side(kids[at, :]))
         return carry
 
-    lax.fori_loop(0, ROWS // CHUNK, turn_kids, 0, unroll=4)
+    for k in range(4):
+        get_kids[k].wait()
+        lax.fori_loop(4 * k, 4 * k + 4, turn_kids, 0, unroll=4)
 
     def pick_kids(a, carry):
         for s in range(4):
@@ -241,12 +256,18 @@
         pltpu.make_async_copy(src.at[others, :], dst.at[others, :], sem).wait()
 
     keep(outbox, inbox, 0).start()
+    def give(k, carry):
+        send(outbox, inbox, 0, lax.rem(me + k * STRIDE, DEVICES))
+        return carry
+
+    lax.fori_loop(1, DEVICES, give, 0)
+
+    for copy in get_small[2:]:
+        copy.wait()
     prepare_hamiltonian(hamiltonian, weights, left)
     get_folks.wait()
 
-    def first_wait(i, count):
-        for n in range(count):
-            send(outbox, inbox, 0, lax.rem(me + (i * 8 + n + 1) * STRIDE, DEVICES))
+    def first_wait(i, carry):
         at = pl.ds(pl.multiple_of(i * CHUNK, CHUNK), CHUNK)
         x = folks[at, :]
         both = side_by_side(x)
@@ -255,8 +276,9 @@
         x = kids[at, :]
         kids_part[at, :] = own_terms(x, side_by_side(x), i * 4, weights, left, damping_s, modes_s, 4)
         pltpu.make_async_copy(kids_part.at[at, :], kids_out.at[at, :], out_sem.at[0]).start()
-
-    chunks(first_wait)
+        return carry
+
+    lax.fori_loop(0, ROWS // CHUNK, first_wait, 0, unroll=4)
 
     def pick_near(a, carry):
         for s in range(4):
@@ -266,6 +288,12 @@
         return carry
 
     lax.fori_loop(0, HALF, pick_near, 0, unroll=4)
+    put_near = [
+        pltpu.make_async_copy(near_row, near_row_out, out_sem.at[2]),
+        pltpu.make_async_copy(near_col, near_col_out, out_sem.at[3]),
+    ]
+    for copy in put_near:
+        copy.start()
 
     lines[:, REQS:] = jnp.where(q_row < HALF, q_row * HALF + mode_row, ROWS)
     for k in range(2):
@@ -322,6 +350,8 @@
     lax.fori_loop(0, ROWS // CHUNK, add_raised, 0, unroll=4)
     wait_others(outbox, inbox, send_sem.at[0])
     wait_others(reply, answers, send_sem.at[1])
+    for copy in put_near:
+        copy.wait()
     pltpu.make_async_copy(kids_part, kids_out, out_sem.at[0]).wait()
     pltpu.make_async_copy(folks_done, folks_out, out_sem.at[1]).wait()
     keep(reply, answers, 1).wait()
@@ -329,15 +359,29 @@
 
 
 def rates_kernel(
-    live_s, modes, source, real, imag, answers, near_row, near_col, kids_part, folks_done,
+    live_s, modes_h, source_h, real_h, imag_h, answers_h, near_row_h, near_col_h, kids_part, folks_done,
     child_out, parent_out,
-    part, done, through, rows, cols, lines, in_sem, out_sem,
+    part, done, through, answers, near_row, near_col, modes, source, real, imag, rows, cols, lines,
+    in_sem, small_sem, out_sem,
 ):
+    get_small = [
+        pltpu.make_async_copy(src, dst, small_sem.at[k])
+        for k, (src, dst) in enumerate(
+            (
+                (modes_h, modes), (source_h, source), (answers_h, answers), (near_row_h, near_row),
+                (near_col_h, near_col), (real_h, real), (imag_h, imag),
+            )
+        )
+    ]
+    for copy in get_small:
+        copy.start()
     get_part = pltpu.make_async_copy(kids_part, part, in_sem.at[0])
     get_part.start()
     get_parents = pltpu.make_async_copy(folks_done, through, in_sem.at[1])
     get_parents.start()
     put_parents = pltpu.make_async_copy(through, parent_out, out_sem.at[0])
+    for copy in get_small[:2]:
+        copy.wait()
 
     q_row, mode_row = slots_row(source[...]), slots_row(modes[...])
     q_col, mode_col = as_column(q_row), as_column(mode_row)
@@ -345,6 +389,8 @@
     spot = jnp.where(owner_col >= 0, owner_col * 8 + rank_col, -8)
     spots = jnp.concatenate([spot, spot + PLACES], axis=0)
     pick = (iota((2 * SLOTS, BOX), 1) == spots).astype(F32).astype(BF16)
+    for copy in get_small[2:]:
+        copy.wait()
     got = dot(pick, side_by_side(answers[...]))
     got = got[:, :LANES] + got[:, LANES:]
     near = owner_col < 0
@@ -397,12 +443,16 @@
     answers, near_row, near_col, kids_part, folks_done = pl.pallas_call(
         exchange_kernel,
         out_shape=(box, lines, lines, whole, whole),
-        in_specs=[SMEM] * 5 + [VMEM] * 4 + [HBM] * 2,
-        out_specs=(HBM, VMEM, VMEM, HBM, HBM),
+        in_specs=[SMEM] * 5 + [HBM] * 6,
+        out_specs=(HBM,) * 5,
         scratch_shapes=[pltpu.VMEM((ROWS, LANES), F32)] * 6
         + [pltpu.VMEM((BOX, LANES), F32)] * 3
-        + [pltpu.VMEM((SLOTS, LANES), F32)] * 2
+        + [pltpu.VMEM((SLOTS, LANES), F32)] * 4
         + [
+            pltpu.VMEM((4, HALF), I32),
+            pltpu.VMEM((4, HALF), I32),
+            pltpu.VMEM((2, DEVICES), I32),
+            pltpu.VMEM((HALF, HALF), F32),
             pltpu.VMEM((8, LANES), I32),
             pltpu.SMEM((8, LANES), I32),
             pltpu.VMEM((2 * LANES, 2 * LANES), BF16),
@@ -411,7 +461,9 @@
             pltpu.VMEM((2 * LANES, every), BF16),
             pltpu.VMEM((1, every), I32),
             pltpu.SemaphoreType.DMA((3,)),
-            pltpu.SemaphoreType.DMA((2,)),
+            pltpu.SemaphoreType.DMA((4,)),
+            pltpu.SemaphoreType.DMA((4,)),
+            pltpu.SemaphoreType.DMA((4,)),
             pltpu.SemaphoreType.DMA((2,)),
             pltpu.SemaphoreType.DMA((2,)),
             pltpu.SemaphoreType.DMA((2,)),
@@ -426,16 +478,24 @@
     child_rates, parent_rates = pl.pallas_call(
         rates_kernel,
         out_shape=(whole, whole),
-        in_specs=[SMEM] + [VMEM] * 7 + [HBM] * 2,
+        in_specs=[SMEM] + [HBM] * 9,
         out_specs=(HBM, HBM),
         scratch_shapes=[
             pltpu.VMEM((ROWS, LANES), F32),
             pltpu.VMEM((ROWS, LANES), F32),
             pltpu.VMEM((ROWS, LANES), F32),
+            pltpu.VMEM((BOX, LANES), F32),
+            pltpu.VMEM((SLOTS, LANES), F32),
+            pltpu.VMEM((SLOTS, LANES), F32),
+            pltpu.VMEM((4, HALF), I32),
+            pltpu.VMEM((4, HALF), I32),
+            pltpu.VMEM((1, HALF), F32),
+            pltpu.VMEM((1, HALF), F32),
             pltpu.VMEM((SLOTS, 2 * LANES), BF16),
             pltpu.VMEM((2 * LANES, SLOTS), BF16),
             pltpu.VMEM((1, SLOTS), I32),
             pltpu.SemaphoreType.DMA((2,)),
+            pltpu.SemaphoreType.DMA((7,)),
             pltpu.SemaphoreType.DMA((2,)),
         ],
         compiler_params=pltpu.CompilerParams(vmem_limit_bytes=60 * 2**20),

time: 45.1 us -> 41.1 us (0.911)
  Pallas kernels: 43.6 us -> 39.7 us
    pallas_call x1, Pallas kernels: 37.3 us -> 34.2 us  [body(): pl.pallas_call(exchange_kernel, out_shape=(box, lines, lines, whole, whol...]
    pallas_call x1, Pallas kernels: 6.28 us -> 5.47 us  [body(): pl.pallas_call(rates_kernel, out_shape=(whole, whole), in_specs=[SMEM] +...]
where the time goes in v3:
time: 41.1 us; the launch traced here: 41 us
  Pallas kernels  39.7 us (97%)
  between operations  1.29 us (3%)
    pallas_call x1, Pallas kernels, body(): pl.pallas_call(exchange_kernel, out_shape=(box, lines, lines, whole, whol...  34.2 us
    pallas_call x1, Pallas kernels, body(): pl.pallas_call(rates_kernel, out_shape=(whole, whole), in_specs=[SMEM] +...  5.47 us

profile of v3, /device:TPU:1, one launch (start us, length us, event | category | flops | bytes accessed | tf_op | source)
XLA Modules:
  0.0 41.0 jit_solution(9153139540506247060)
XLA Ops:
  1.3 34.2 %shard_map.122 = (f32[1024,128]{1,0:T(8,128)}, f32[256,128]{1,0:T(8,128)}, f32[256,128]{1,0:T(8,128)}, f32[4096,128]{1,0:T(8,128)}, f32[4096,128]{1,0:T(8,128)}) custom-call(s32[4,64]{1,0:T(4,128)} %bitcast.14, s32[4,64]{1,0:T(4,128)} %bitcast.17, s32[3,64]{1,0:T(4,128)} %bitcast.20, s32[1]{0:T(128)S(6)} %copy.13.live_s, f32[64]{0:T(128)} %damping_s.1, ...), custom_call_target="tpu_custom_call" | custom-call | tf_op jit(solution)/shard_map/pallas_call | solution.py:443
  35.5 5.5 %shard_map.123 = (f32[4096,128]{1,0:T(8,128)}, f32[4096,128]{1,0:T(8,128)}) custom-call(s32[1]{0:T(128)S(6)} %copy.13.live_s, s32[4,64]{1,0:T(4,128)} %bitcast.16, s32[4,64]{1,0:T(4,128)} %bitcast.19, f32[1,64]{1,0:T(1,128)} %bitcast.22, f32[1,64]{1,0:T(1,128)} %bitcast.23, f32[1024,128]{1,0:T(8,128)} %get-tuple-element.9.answers_h, ...), custom_call_target="tpu_custom_call" | custom-call | tf_op jit(solution)/shard_map/pallas_call | solution.py:478
